TPU v7x, 256 devices: a whole 4x4x8 slice. The times are simulated.
256 devices in a mesh: group: 4 (over y), region: 64 (over x, z, core).
Axes of the slice: x: 4, y: 4, z: 8, core: 2. Of those that a mesh axis runs over, the one named last changes fastest.
Arguments:
- position: float32 [3, 262144], P(None, ('group', 'region')), may hold values from -6 to 6
- velocity: float32 [3, 262144], P(None, ('group', 'region')), may hold values from -6 to 6
- accel_old: float32 [3, 262144], P(None, ('group', 'region')), may hold values from -6 to 6
- orientation: float32 [9, 262144], P(None, ('group', 'region')), may hold values from -3.5 to 3.5
- spin: float32 [3, 262144], P(None, ('group', 'region')), may hold values from -6 to 6
- shape_index: int32 [262144], P(('group', 'region')), may hold values from 0 to 63
- shape_offsets: float32 [64, 3, 128], replicated, may hold values from -3 to 3
- shape_radii: float32 [64, 128], replicated, may hold values from 0.2 to 0.6
- pair_first: int32 [32768], P(('group', 'region')), may hold values from 0 to 1023
- pair_second: int32 [32768], P(('group', 'region')), may hold values from 0 to 1278
- pair_neck: float32 [32768], P(('group', 'region')), may hold values from 0.05 to 0.5
- cross_first: int32 [16384], P(('group', 'region')), may hold values from 0 to 1023
- cross_second: int32 [16384], P(('group', 'region')), may hold values from 0 to 127
- cross_neck: float32 [16384], P(('group', 'region')), may hold values from 0.05 to 0.5
- export_slots: int32 [32768], P(('group', 'region')), may hold values from 0 to 1023
Outputs:
- moved: float32 [3, 262144], P(None, ('group', 'region'))
- velocity_new: float32 [3, 262144], P(None, ('group', 'region'))
- spin_new: float32 [3, 262144], P(None, ('group', 'region'))
All inputs are finite; a program needn't handle non-finite values.
Results may differ from a plain program's by a relative error of at most 0.00002.
Values sent between devices are 32-bit elements; how exact they have to be, the bound alone decides.
No kernel may reach another device: no remote copies, remote signals or barrier semaphores. Data moves between devices by JAX's collectives and lax.ppermute only.
A program may use at most 64 MiB of HBM per device.

v0:
```python
import math

import jax
import jax.numpy as jnp
from jax import lax
from jax.sharding import PartitionSpec as P

BOUND_DEV = 128
CX = 32


time_step = 0.05
stiffness = 0.0078125
cohesion = 0.05
inertia = 0.4


def with_halo(array, sides, width):
    for axis, dim in sides:
        devices, length = (lax.axis_size(axis), array.shape[dim])
        up = [(i, (i + 1) % devices) for i in range(devices)]
        down = [(j, i) for i, j in up]
        last = lax.slice_in_dim(array, length - width, length, axis=dim)
        initial = lax.slice_in_dim(array, 0, width, axis=dim)
        before = lax.ppermute(last, axis, up)
        after = lax.ppermute(initial, axis, down)
        array = jnp.concatenate([before, array, after], axis=dim)
    return array


def from_behind(array, axis, by):
    devices = lax.axis_size(axis)
    return lax.ppermute(array, axis, [(i, (i + by) % devices) for i in range(devices)])


def build(centre, turn, chosen):
    offsets = chosen[:, :3]
    rows = []
    for c in range(3):
        value = centre[c][:, None] + turn[3 * c][:, None] * offsets[:, 0]
        value = value + turn[3 * c + 1][:, None] * offsets[:, 1]
        value = value + turn[3 * c + 2][:, None] * offsets[:, 2]
        rows.append(value)
    rows.append(chosen[:, 3])
    return jnp.stack(rows, 1)


def crossed(left, right):
    return jnp.stack(
        [
            left[:, 1] * right[:, 2] - left[:, 2] * right[:, 1],
            left[:, 2] * right[:, 0] - left[:, 0] * right[:, 2],
            left[:, 0] * right[:, 1] - left[:, 1] * right[:, 0],
        ],
        1,
    )


def tile(world_i, centre_i, world_j, centre_j, neck):
    delta = world_i[:, :3, :, None] - world_j[:, :3, None, :]
    square = delta[:, 0] ** 2 + delta[:, 1] ** 2 + delta[:, 2] ** 2
    spacing = jnp.sqrt(square + 0.01)
    reach = world_i[:, 3, :, None] + world_j[:, 3, None, :]
    magnitude = (
        (stiffness * (reach - spacing) - cohesion * neck[:, None, None])
        * jnp.exp(-square * 0.25)
        / spacing
    )
    pushes = magnitude[:, None] * delta
    along_i = jnp.sum(pushes, 3)
    along_j = jnp.sum(pushes, 2)
    force_i = jnp.sum(along_i, 2)
    torque_i = jnp.sum(crossed(world_i[:, :3] - centre_i[:, :, None], along_i), 2)
    torque_j = -jnp.sum(crossed(world_j[:, :3] - centre_j[:, :, None], along_j), 2)
    return (jnp.concatenate([force_i, torque_i], 1), jnp.concatenate([-force_i, torque_j], 1))


def lookup(kinds, table):
    return jnp.take(table, kinds, 0)


def spread(terms, index, count):
    return jax.ops.segment_sum(terms, index, num_segments=count).T


def pair_loop(first, second, neck, local_flat, centres, fetch):
    total = first.shape[0]
    block = math.gcd(total, 32)
    sub_count = local_flat.shape[1] // 4

    def work(pieces):
        one, two, strength = pieces
        world_i = jnp.take(local_flat, one, 0)
        centre_i = jnp.take(centres, one, 0)
        world_j, centre_j = fetch(two)
        return tile(world_i.reshape(-1, 4, sub_count), centre_i, world_j, centre_j, strength)

    terms_i, terms_j = lax.map(
        work, (first.reshape(-1, block), second.reshape(-1, block), neck.reshape(-1, block))
    )
    return (terms_i.reshape(total, 6), terms_j.reshape(total, 6))


def on_device(
    position,
    velocity,
    accel_old,
    orientation,
    spin,
    shape_index,
    shape_offsets,
    shape_radii,
    pair_first,
    pair_second,
    pair_neck,
    cross_first,
    cross_second,
    cross_neck,
    export_slots,
):
    count = position.shape[1]
    groups = lax.axis_size("group")
    bound = BOUND_DEV
    sub_count = shape_offsets.shape[2]
    moved = position + time_step * velocity + 0.5 * time_step**2 * accel_old
    table = jnp.concatenate([shape_offsets, shape_radii[:, None, :]], 1)
    local_world = build(moved, orientation, lookup(shape_index, table))
    centres = moved.T
    poses = jnp.concatenate([moved, orientation], 0)
    centre_rows = jnp.pad(moved[:, :bound].T[:, None, :], ((0, 0), (0, 0), (0, sub_count - 3)))
    packed = jnp.concatenate([local_world[:bound], centre_rows], 1)
    extended = with_halo(packed, (("region", 0),), bound)
    near = jnp.concatenate([extended[:bound], extended[2 * bound :]], 0)
    near_world = near[:, :4]
    near_centre = near[:, 4, :3]
    local_flat = local_world.reshape(count, 4 * sub_count)
    all_flat = jnp.concatenate([local_flat, near_world.reshape(2 * bound, 4 * sub_count)], 0)
    all_centre = jnp.concatenate([centres, near_centre], 0)
    partner = jnp.where(
        pair_second < count - 1, (pair_first + 1 + pair_second) % count, pair_second + 1
    )

    def fetch_near(index):
        world_j = jnp.take(all_flat, index, 0)
        centre_j = jnp.take(all_centre, index, 0)
        return (world_j.reshape(-1, 4, sub_count), centre_j)

    sent_poses = jnp.take(poses, export_slots, 1).T
    sent_kinds = jnp.take(shape_index, export_slots, 0)
    got_poses, got_kinds = (
        lax.all_to_all(sent_poses, "group", split_axis=0, concat_axis=0, tiled=True),
        lax.all_to_all(sent_kinds, "group", split_axis=0, concat_axis=0, tiled=True),
    )

    def fetch_cross(index):
        chosen = jnp.take(got_poses, index, 0).T
        kinds = jnp.take(got_kinds, index, 0)
        return (build(chosen[:3], chosen[3:], lookup(kinds, table)), chosen[:3].T)

    inner_i, inner_j = pair_loop(pair_first, partner, pair_neck, local_flat, centres, fetch_near)
    outer_i, outer_j = pair_loop(
        cross_first, cross_second, cross_neck, local_flat, centres, fetch_cross
    )
    totals = spread(
        jnp.concatenate([inner_i, outer_i], 0), jnp.concatenate([pair_first, cross_first]), count
    )
    near_terms = spread(inner_j, partner, count + 2 * bound)
    totals = totals + near_terms[:, :count]
    from_next = from_behind(near_terms[:, count : count + bound], "region", -1)
    from_prev = from_behind(near_terms[:, count + bound :], "region", 1)
    totals = totals + jnp.pad(from_next + from_prev, ((0, 0), (0, count - bound)))
    cross_terms = spread(outer_j, cross_second, groups * CX)
    returned = lax.all_to_all(cross_terms, "group", split_axis=1, concat_axis=1, tiled=True)
    totals = totals + spread(returned.T, export_slots, count)
    force = totals[:3]
    torque = totals[3:]
    velocity_new = velocity + 0.5 * time_step * (accel_old + force)
    spin_new = spin + time_step * torque / inertia
    return (moved, velocity_new, spin_new)


def solution(mesh):
    in_specs = (
        P(None, ("group", "region")),
        P(None, ("group", "region")),
        P(None, ("group", "region")),
        P(None, ("group", "region")),
        P(None, ("group", "region")),
        P(("group", "region")),
        P(),
        P(),
        P(("group", "region")),
        P(("group", "region")),
        P(("group", "region")),
        P(("group", "region")),
        P(("group", "region")),
        P(("group", "region")),
        P(("group", "region")),
    )
    out_specs = (
        P(None, ("group", "region")),
        P(None, ("group", "region")),
        P(None, ("group", "region")),
    )
    return jax.shard_map(
        on_device, mesh=mesh, in_specs=in_specs, out_specs=out_specs, check_vma=False
    )
```

profile of v0, /device:TPU:8, one launch (start us, length us, event | category | flops | bytes accessed | tf_op | source)
XLA Modules:
  0.0 174.6 jit_solution(12883599754519796214)
XLA Ops:
  0.6 0.8 multiply_add_fusion.6
  1.4 1.1 fusion.33
  2.5 1.0 copy.352
  5.5 0.8 pad_maximum_fusion.4
  6.4 3.6 %gather_fusion.9 = f32[1024,4,128]{2,1,0:T(4,128)S(1)} fusion(f32[64,4,128]{2,1,0:T(4,128)S(1)} %pad_maximum_fusion.4, s32[1024]{0:T(1024)S(1)} %get-tuple-element.468), kind=kCustom, calls=%fused_computation.9 | custom fusion | bytes 4198400 | tf_op jit(solution)/shard_map/jit(_take)/gather | solution.py:79
  10.2 0.8 multiply_add_fusion.3
  11.1 1.3 multiply_add_fusion.5
  12.6 1.3 copy-done.1
  14.0 0.7 select_maximum_fusion
  14.8 7.5 %collective-permute-start.1 = (f32[128,5,128]{2,0,1:T(8,128)}, f32[128,5,128]{2,0,1:T(8,128)}, u32[]{:S(2)}, u32[]{:S(2)}) collective-permute-start(f32[128,5,128]{2,0,1:T(8,128)} %select_maximum_fusion), channel_id=1, source_target_pairs={{1,0},{2,1},{3,2},{4,3},{5,4},{6,5},{7,6},{8,7},{9,8},{10,9},{11,1... | collective-permute-start | bytes 983048 | tf_op jit(solution)/shard_map/ppermute | solution.py:26
  22.2 1.0 gather_fusion.10
  23.9 4.9 %all-to-all-start = ((s32[4,32,1]{1,2,0:T(1,128)}), s32[4,32,1]{1,2,0:T(1,128)S(1)}, u32[]{:S(2)}, u32[]{:S(2)}) async-start(s32[4,32,1]{1,2,0:T(1,128)} %bitcast.43), calls=%async_computation | async-start | bytes 4096 | tf_op jit(solution)/shard_map/all_to_all | solution.py:152
  31.0 1.5 all-to-all-done
  32.5 4.7 %all-to-all-start.1 = ((f32[4,1,384]{2,1,0:T(1,128)}), f32[4,1,384]{2,1,0:T(1,128)S(1)}, u32[]{:S(2)}, u32[]{:S(2)}) async-start(f32[4,1,384]{2,1,0:T(1,128)} %reshape.641), calls=%async_computation.1 | async-start | bytes 12288 | tf_op jit(solution)/shard_map/all_to_all | solution.py:151
  37.2 2.9 %copy.354 = f32[1024,4,128]{0,2,1:T(8,128)} copy(f32[1024,4,128]{2,0,1:T(8,128)} %copy-done.1) | data formatting | bytes 4194304 | tf_op jit(solution)/shard_map/stack | solution.py:45
  40.2 2.0 %copy.358 = f32[1024,512]{1,0:T(8,128)S(1)} copy(f32[1024,512]{0,1:T(8,128)} %bitcast.158) | data formatting | bytes 4194304 | tf_op jit(solution)/shard_map/while | solution.py:98
  45.3 26.9 %while.25 = (s32[]{:T(128)}, f32[2,32,6]{1,0,2:T(2,128)S(1)}, f32[2,32,6]{1,2,0:T(8,128)S(1)}, s32[2,32]{1,0:T(2,128)S(1)}, f32[1024,512]{1,0:T(8,128)S(1)}, /*i...) while((s32[]{:T(128)}, f32[2,32,6]{1,0,2:T(2,128)S(1)}, ...), condition=%wide.region_13.16_spmd, body=%wide.region_7.15_spmd.sunk | while | flops 17060640 | bytes 18905076 | solution.py:98
  45.4 0.7 gather_fusion.5
  49.8 1.8 %broadcast_subtract_fusion.13 = f32[32,3,128,128]{3,2,1,0:T(8,128)S(1)} fusion(f32[32,3,128]{2,1,0:T(4,128)S(1)} %copy.418, f32[32,3,128]{2,1,0:T(4,128)S(1)} %get-tuple-element.683), kind=kLoop, calls=%fused_computation.60.clone.1 | loop fusion | flops 1572864 | bytes 6389760 | tf_op jit(solution)/shard_map/while/body/eval_jaxpr/sub | solution.py:60
  51.6 1.9 %divide_bitcast_fusion.5 = f32[32,128,128]{2,1,0:T(8,128)S(1)} fusion(f32[32,3,128,128]{3,2,1,0:T(8,128)S(1)} %broadcast_subtract_fusion.13, f32[32]{0:T(128)S(1)} %fusion.53, f32[32,128]{1,0:T(8,128)S(1)} %get-tuple-element.684, f32[32,128]{1,0:T(8,128)S(1)} %bitcast.163), kind=kLoop, calls=%fused_computation.66.clone.1 | loop fusion | flops 7340032 | bytes 8421504 | tf_op jit(solution)/shard_map/while/body/eval_jaxpr/mul | solution.py:69
  53.5 4.7 %multiply_reduce_fusion.9 = (f32[32,3,128]{2,1,0:T(4,128)S(1)}, f32[32,3,128]{2,1,0:T(4,128)S(1)}, f32[32,3]{1,0:T(8,128)S(1)}) fusion(f32[32,128,128]{2,1,0:T(8,128)S(1)} %divide_bitcast_fusion.5, f32[32,3,128]{2,1,0:T(4,128)S(1)} %copy.418, f32[32,3,128]{2,1,0:T(4,128)S(1)} %get-tuple-element.683), kind=kLoop, calls=%fused_computation.57.clone.1 | loop fusion | flops 7839648 | bytes 2294144 | tf_op jit(solution)/shard_map/while/body/eval_jaxpr/reduce_sum | solution.py:71
  58.8 0.7 gather_fusion.5
  63.2 1.8 %broadcast_subtract_fusion.13 = f32[32,3,128,128]{3,2,1,0:T(8,128)S(1)} fusion(f32[32,3,128]{2,1,0:T(4,128)S(1)} %copy.418, f32[32,3,128]{2,1,0:T(4,128)S(1)} %get-tuple-element.683), kind=kLoop, calls=%fused_computation.60.clone.1 | loop fusion | flops 1572864 | bytes 6389760 | tf_op jit(solution)/shard_map/while/body/eval_jaxpr/sub | solution.py:60
  65.1 1.9 %divide_bitcast_fusion.5 = f32[32,128,128]{2,1,0:T(8,128)S(1)} fusion(f32[32,3,128,128]{3,2,1,0:T(8,128)S(1)} %broadcast_subtract_fusion.13, f32[32]{0:T(128)S(1)} %fusion.53, f32[32,128]{1,0:T(8,128)S(1)} %get-tuple-element.684, f32[32,128]{1,0:T(8,128)S(1)} %bitcast.163), kind=kLoop, calls=%fused_computation.66.clone.1 | loop fusion | flops 7340032 | bytes 8421504 | tf_op jit(solution)/shard_map/while/body/eval_jaxpr/mul | solution.py:69
  66.9 4.7 %multiply_reduce_fusion.9 = (f32[32,3,128]{2,1,0:T(4,128)S(1)}, f32[32,3,128]{2,1,0:T(4,128)S(1)}, f32[32,3]{1,0:T(8,128)S(1)}) fusion(f32[32,128,128]{2,1,0:T(8,128)S(1)} %divide_bitcast_fusion.5, f32[32,3,128]{2,1,0:T(4,128)S(1)} %copy.418, f32[32,3,128]{2,1,0:T(4,128)S(1)} %get-tuple-element.683), kind=kLoop, calls=%fused_computation.57.clone.1 | loop fusion | flops 7839648 | bytes 2294144 | tf_op jit(solution)/shard_map/while/body/eval_jaxpr/reduce_sum | solution.py:71
  72.3 0.8 scatter_custom_fusion.2
  74.0 4.8 %all-to-all-start.2 = ((f32[4,1,192]{2,1,0:T(1,128)}), f32[4,1,192]{2,1,0:T(1,128)S(1)}, u32[]{:S(2)}, u32[]{:S(2)}) async-start(f32[4,1,192]{2,1,0:T(1,128)} %reshape.643), calls=%async_computation.2 | async-start | bytes 8192 | tf_op jit(solution)/shard_map/all_to_all | solution.py:173
  81.4 1.2 all-to-all-done.2
  83.5 1.4 scatter_custom_fusion.3
  85.0 0.8 copy.382
  85.8 1.0 constant_dynamic-update-slice_fusion.1
  86.8 1.0 constant_dynamic-update-slice_fusion
  87.8 0.8 slice.409
  88.6 1.2 copy.356
  89.9 3.3 %pad_maximum_fusion.1 = f32[1280,512]{0,1:T(8,128)} fusion(f32[256,512]{0,1:T(8,128)S(1)} %bitcast.161, f32[1024,512]{0,1:T(8,128)} %bitcast.159), kind=kLoop, calls=%fused_computation.122 | loop fusion | flops 655360 | bytes 5242880 | tf_op jit(solution)/shard_map/concatenate | solution.py:137
  93.2 3.2 %copy.359 = f32[1280,512]{1,0:T(8,128)} copy(f32[1280,512]{0,1:T(8,128)} %pad_maximum_fusion.1) | data formatting | bytes 5242880 | tf_op jit(solution)/shard_map/while | solution.py:98
  96.5 1.1 copy.361
  97.7 68.1 %while.24 = (s32[]{:T(128)}, f32[4,32,6]{1,0,2:T(4,128)S(1)}, f32[4,32,6]{1,2,0:T(8,128)S(1)}, s32[4,32]{1,0:T(4,128)}, f32[1024,512]{1,0:T(8,128)S(1)}, /*index...) while((s32[]{:T(128)}, f32[4,32,6]{1,0,2:T(4,128)S(1)}, ...), condition=%wide.region_6.9_spmd, body=%wide.region_0.8_spmd.sunk | while | flops 16960480 | bytes 18676936 | solution.py:98
  100.5 2.4 %gather_fusion.1 = f32[32,512]{1,0:T(8,128)S(1)} fusion(f32[1280,512]{1,0:T(8,128)} %get-tuple-element.729, s32[1024]{0:T(1024)S(1)} %pad_clamp_fusion.11), kind=kCustom, calls=%fused_computation.2.clone.1 | custom fusion | bytes 131200 | tf_op jit(solution)/shard_map/while/body/eval_jaxpr/jit(_take)/gather | solution.py:144
  103.0 1.7 gather_fusion
  104.9 1.8 %broadcast_subtract_fusion.11 = f32[32,3,128,128]{3,2,1,0:T(8,128)S(1)} fusion(f32[32,3,128]{2,1,0:T(4,128)S(1)} %get-tuple-element.638, f32[32,3,128]{2,1,0:T(4,128)S(1)} %get-tuple-element.641), kind=kLoop, calls=%fused_computation.19.clone.1 | loop fusion | flops 1572864 | bytes 6389760 | tf_op jit(solution)/shard_map/while/body/eval_jaxpr/sub | solution.py:60
  107.4 1.8 %divide_bitcast_fusion.4 = f32[32,128,128]{2,1,0:T(8,128)S(1)} fusion(f32[32,3,128,128]{3,2,1,0:T(8,128)S(1)} %broadcast_subtract_fusion.11, f32[32]{0:T(128)S(1)} %fusion.48, f32[32,128]{1,0:T(8,128)S(1)} %bitcast.164, f32[32,128]{1,0:T(8,128)S(1)} %bitcast.162), kind=kLoop, calls=%fused_computation.25.clone.1 | loop fusion | flops 7340032 | bytes 8421504 | tf_op jit(solution)/shard_map/while/body/eval_jaxpr/mul | solution.py:69
  109.2 4.7 %multiply_reduce_fusion.8 = (f32[32,3,128]{2,1,0:T(4,128)S(1)}, f32[32,3,128]{2,1,0:T(4,128)S(1)}, f32[32,3]{1,0:T(8,128)S(1)}) fusion(f32[32,128,128]{2,1,0:T(8,128)S(1)} %divide_bitcast_fusion.4, f32[32,3,128]{2,1,0:T(4,128)S(1)} %get-tuple-element.638, f32[32,3,128]{2,1,0:T(4,128)S(1)} %get-tuple-element.641), kind=kLoop, calls=%fused_computation.16.clone.1 | loop fusion | flops 7839648 | bytes 2294144 | tf_op jit(solution)/shard_map/while/body/eval_jaxpr/reduce_sum | solution.py:71
  114.7 0.7 compare_and_fusion.11
  117.6 2.4 %gather_fusion.1 = f32[32,512]{1,0:T(8,128)S(1)} fusion(f32[1280,512]{1,0:T(8,128)} %get-tuple-element.729, s32[1024]{0:T(1024)S(1)} %pad_clamp_fusion.11), kind=kCustom, calls=%fused_computation.2.clone.1 | custom fusion | bytes 131200 | tf_op jit(solution)/shard_map/while/body/eval_jaxpr/jit(_take)/gather | solution.py:144
  120.1 1.7 gather_fusion
  121.9 1.8 %broadcast_subtract_fusion.11 = f32[32,3,128,128]{3,2,1,0:T(8,128)S(1)} fusion(f32[32,3,128]{2,1,0:T(4,128)S(1)} %get-tuple-element.638, f32[32,3,128]{2,1,0:T(4,128)S(1)} %get-tuple-element.641), kind=kLoop, calls=%fused_computation.19.clone.1 | loop fusion | flops 1572864 | bytes 6389760 | tf_op jit(solution)/shard_map/while/body/eval_jaxpr/sub | solution.py:60
  124.4 1.8 %divide_bitcast_fusion.4 = f32[32,128,128]{2,1,0:T(8,128)S(1)} fusion(f32[32,3,128,128]{3,2,1,0:T(8,128)S(1)} %broadcast_subtract_fusion.11, f32[32]{0:T(128)S(1)} %fusion.48, f32[32,128]{1,0:T(8,128)S(1)} %bitcast.164, f32[32,128]{1,0:T(8,128)S(1)} %bitcast.162), kind=kLoop, calls=%fused_computation.25.clone.1 | loop fusion | flops 7340032 | bytes 8421504 | tf_op jit(solution)/shard_map/while/body/eval_jaxpr/mul | solution.py:69
  126.3 4.7 %multiply_reduce_fusion.8 = (f32[32,3,128]{2,1,0:T(4,128)S(1)}, f32[32,3,128]{2,1,0:T(4,128)S(1)}, f32[32,3]{1,0:T(8,128)S(1)}) fusion(f32[32,128,128]{2,1,0:T(8,128)S(1)} %divide_bitcast_fusion.4, f32[32,3,128]{2,1,0:T(4,128)S(1)} %get-tuple-element.638, f32[32,3,128]{2,1,0:T(4,128)S(1)} %get-tuple-element.641), kind=kLoop, calls=%fused_computation.16.clone.1 | loop fusion | flops 7839648 | bytes 2294144 | tf_op jit(solution)/shard_map/while/body/eval_jaxpr/reduce_sum | solution.py:71
  131.7 0.7 compare_and_fusion.11
  134.6 2.4 %gather_fusion.1 = f32[32,512]{1,0:T(8,128)S(1)} fusion(f32[1280,512]{1,0:T(8,128)} %get-tuple-element.729, s32[1024]{0:T(1024)S(1)} %pad_clamp_fusion.11), kind=kCustom, calls=%fused_computation.2.clone.1 | custom fusion | bytes 131200 | tf_op jit(solution)/shard_map/while/body/eval_jaxpr/jit(_take)/gather | solution.py:144
  137.1 1.7 gather_fusion
  138.9 1.8 %broadcast_subtract_fusion.11 = f32[32,3,128,128]{3,2,1,0:T(8,128)S(1)} fusion(f32[32,3,128]{2,1,0:T(4,128)S(1)} %get-tuple-element.638, f32[32,3,128]{2,1,0:T(4,128)S(1)} %get-tuple-element.641), kind=kLoop, calls=%fused_computation.19.clone.1 | loop fusion | flops 1572864 | bytes 6389760 | tf_op jit(solution)/shard_map/while/body/eval_jaxpr/sub | solution.py:60
  141.5 1.8 %divide_bitcast_fusion.4 = f32[32,128,128]{2,1,0:T(8,128)S(1)} fusion(f32[32,3,128,128]{3,2,1,0:T(8,128)S(1)} %broadcast_subtract_fusion.11, f32[32]{0:T(128)S(1)} %fusion.48, f32[32,128]{1,0:T(8,128)S(1)} %bitcast.164, f32[32,128]{1,0:T(8,128)S(1)} %bitcast.162), kind=kLoop, calls=%fused_computation.25.clone.1 | loop fusion | flops 7340032 | bytes 8421504 | tf_op jit(solution)/shard_map/while/body/eval_jaxpr/mul | solution.py:69
  143.3 4.7 %multiply_reduce_fusion.8 = (f32[32,3,128]{2,1,0:T(4,128)S(1)}, f32[32,3,128]{2,1,0:T(4,128)S(1)}, f32[32,3]{1,0:T(8,128)S(1)}) fusion(f32[32,128,128]{2,1,0:T(8,128)S(1)} %divide_bitcast_fusion.4, f32[32,3,128]{2,1,0:T(4,128)S(1)} %get-tuple-element.638, f32[32,3,128]{2,1,0:T(4,128)S(1)} %get-tuple-element.641), kind=kLoop, calls=%fused_computation.16.clone.1 | loop fusion | flops 7839648 | bytes 2294144 | tf_op jit(solution)/shard_map/while/body/eval_jaxpr/reduce_sum | solution.py:71
  148.7 0.7 compare_and_fusion.11
  151.6 2.4 %gather_fusion.1 = f32[32,512]{1,0:T(8,128)S(1)} fusion(f32[1280,512]{1,0:T(8,128)} %get-tuple-element.729, s32[1024]{0:T(1024)S(1)} %pad_clamp_fusion.11), kind=kCustom, calls=%fused_computation.2.clone.1 | custom fusion | bytes 131200 | tf_op jit(solution)/shard_map/while/body/eval_jaxpr/jit(_take)/gather | solution.py:144
  154.1 1.7 gather_fusion
  156.0 1.8 %broadcast_subtract_fusion.11 = f32[32,3,128,128]{3,2,1,0:T(8,128)S(1)} fusion(f32[32,3,128]{2,1,0:T(4,128)S(1)} %get-tuple-element.638, f32[32,3,128]{2,1,0:T(4,128)S(1)} %get-tuple-element.641), kind=kLoop, calls=%fused_computation.19.clone.1 | loop fusion | flops 1572864 | bytes 6389760 | tf_op jit(solution)/shard_map/while/body/eval_jaxpr/sub | solution.py:60
  158.5 1.8 %divide_bitcast_fusion.4 = f32[32,128,128]{2,1,0:T(8,128)S(1)} fusion(f32[32,3,128,128]{3,2,1,0:T(8,128)S(1)} %broadcast_subtract_fusion.11, f32[32]{0:T(128)S(1)} %fusion.48, f32[32,128]{1,0:T(8,128)S(1)} %bitcast.164, f32[32,128]{1,0:T(8,128)S(1)} %bitcast.162), kind=kLoop, calls=%fused_computation.25.clone.1 | loop fusion | flops 7340032 | bytes 8421504 | tf_op jit(solution)/shard_map/while/body/eval_jaxpr/mul | solution.py:69
  160.3 4.7 %multiply_reduce_fusion.8 = (f32[32,3,128]{2,1,0:T(4,128)S(1)}, f32[32,3,128]{2,1,0:T(4,128)S(1)}, f32[32,3]{1,0:T(8,128)S(1)}) fusion(f32[32,128,128]{2,1,0:T(8,128)S(1)} %divide_bitcast_fusion.4, f32[32,3,128]{2,1,0:T(4,128)S(1)} %get-tuple-element.638, f32[32,3,128]{2,1,0:T(4,128)S(1)} %get-tuple-element.641), kind=kLoop, calls=%fused_computation.16.clone.1 | loop fusion | flops 7839648 | bytes 2294144 | tf_op jit(solution)/shard_map/while/body/eval_jaxpr/reduce_sum | solution.py:71
  165.9 1.3 scatter_custom_fusion.1
  168.2 1.5 scatter_custom_fusion
  169.9 4.0 %collective-permute-done.3 = f32[6,128]{1,0:T(8,128)S(1)} collective-permute-done((f32[6,128]{1,0:T(8,128)S(1)}, f32[6,128]{1,0:T(8,128)S(1)}, u32[]{:S(2)}, u32[]{:S(2)}) %collective-permute-start.3) | collective-permute-done | bytes 3104 | tf_op jit(solution)/shard_map/ppermute | solution.py:33
  (295 shorter events, 39.8 us)
Async XLA Ops:
  1.4 40.8 %copy-start.2 = (f32[3,1024]{1,0:T(4,128)}, f32[3,1024]{1,0:T(4,128)S(1)}, u32[]{:S(2)}) copy-start(f32[3,1024]{1,0:T(4,128)S(1)} %multiply_add_fusion.6) | copy-start | bytes 36868
  12.4 9.9 %copy-start = (s32[1024]{0:T(1024)S(1)}, s32[1024]{0:T(1024)}, u32[]{:S(2)}) copy-start(s32[1024]{0:T(1024)} %param.28) | copy-start | bytes 12292
  12.4 10.8 %copy-start.14 = (s32[128]{0:T(128)S(1)}, s32[128]{0:T(128)}, u32[]{:S(2)}) copy-start(s32[128]{0:T(128)} %param.37) | copy-start | bytes 1540
  12.6 1.3 copy-start.1
  13.9 15.2 %copy-start.4 = (f32[9,1024]{1,0:T(8,128)S(1)}, f32[9,1024]{1,0:T(8,128)}, u32[]{:S(2)}) copy-start(f32[9,1024]{1,0:T(8,128)} %param.26) | copy-start | bytes 110596
  14.0 23.2 %copy-start.10 = (s32[128]{0:T(128)S(1)}, s32[128]{0:T(128)}, u32[]{:S(2)}) copy-start(s32[128]{0:T(128)} %param.31) | copy-start | bytes 1540
  14.0 23.2 %copy-start.15 = (s32[128]{0:T(128)S(1)}, s32[128]{0:T(128)}, u32[]{:S(2)}) copy-start(s32[128]{0:T(128)} %param.32) | copy-start | bytes 1540
  14.8 71.0 %collective-permute-start = (f32[128,5,128]{2,0,1:T(8,128)}, f32[128,5,128]{2,0,1:T(8,128)}, u32[]{:S(2)}, u32[]{:S(2)}) collective-permute-start(f32[128,5,128]{2,0,1:T(8,128)} %select_maximum_fusion), channel_id=1, source_target_pairs={{0,1},{1,2},{2,3},{3,4},{4,5},{5,6},{6,7},{7,8},{8,9},{9,10},{10,1... | collective-permute-start | bytes 983048 | tf_op jit(solution)/shard_map/ppermute | solution.py:25
  14.8 72.0 %collective-permute-start.1 = (f32[128,5,128]{2,0,1:T(8,128)}, f32[128,5,128]{2,0,1:T(8,128)}, u32[]{:S(2)}, u32[]{:S(2)}) collective-permute-start(f32[128,5,128]{2,0,1:T(8,128)} %select_maximum_fusion), channel_id=1, source_target_pairs={{1,0},{2,1},{3,2},{4,3},{5,4},{6,5},{7,6},{8,7},{9,8},{10,9},{11,1... | collective-permute-start | bytes 983048 | tf_op jit(solution)/shard_map/ppermute | solution.py:26
  23.9 8.6 %all-to-all-start = ((s32[4,32,1]{1,2,0:T(1,128)}), s32[4,32,1]{1,2,0:T(1,128)S(1)}, u32[]{:S(2)}, u32[]{:S(2)}) async-start(s32[4,32,1]{1,2,0:T(1,128)} %bitcast.43), calls=%async_computation | async-start | bytes 4096 | tf_op jit(solution)/shard_map/all_to_all | solution.py:152
  32.5 11.4 %all-to-all-start.1 = ((f32[4,1,384]{2,1,0:T(1,128)}), f32[4,1,384]{2,1,0:T(1,128)S(1)}, u32[]{:S(2)}, u32[]{:S(2)}) async-start(f32[4,1,384]{2,1,0:T(1,128)} %reshape.641), calls=%async_computation.1 | async-start | bytes 12288 | tf_op jit(solution)/shard_map/all_to_all | solution.py:151
  37.2 42.8 %copy-start.12 = (s32[128]{0:T(128)}, s32[128]{0:T(128)S(1)}, u32[]{:S(2)}) copy-start(s32[128]{0:T(128)S(1)} %compare_select_fusion.12) | copy-start | bytes 1540
  40.2 2.2 %copy-start.13 = (s32[64]{0:T(128)S(1)}, s32[64]{0:T(128)}, u32[]{:S(2)}) copy-start(s32[64]{0:T(128)} %param.34) | copy-start | bytes 772
  40.2 2.3 %copy-start.17 = (s32[64]{0:T(128)S(1)}, s32[64]{0:T(128)}, u32[]{:S(2)}) copy-start(s32[64]{0:T(128)} %param.35) | copy-start | bytes 772
  40.2 2.4 %copy-start.16 = (f32[64]{0:T(128)S(1)}, f32[64]{0:T(128)}, u32[]{:S(2)}) copy-start(f32[64]{0:T(128)} %param.36) | copy-start | bytes 772
  45.3 35.3 %copy-start.11 = (f32[128]{0:T(128)S(1)}, f32[128]{0:T(128)}, u32[]{:S(2)}) copy-start(f32[128]{0:T(128)} %param.33) | copy-start | bytes 1540
  74.0 8.6 %all-to-all-start.2 = ((f32[4,1,192]{2,1,0:T(1,128)}), f32[4,1,192]{2,1,0:T(1,128)S(1)}, u32[]{:S(2)}, u32[]{:S(2)}) async-start(f32[4,1,192]{2,1,0:T(1,128)} %reshape.643), calls=%async_computation.2 | async-start | bytes 8192 | tf_op jit(solution)/shard_map/all_to_all | solution.py:173
  93.2 3.3 %copy-start.3 = (f32[3,1024]{1,0:T(4,128)S(1)}, f32[3,1024]{1,0:T(4,128)}, u32[]{:S(2)}) copy-start(f32[3,1024]{1,0:T(4,128)} %copy-done.2) | copy-start | bytes 36868
  93.2 4.5 %copy-start.9 = (f32[4,32,6]{1,2,0:T(8,128)S(1)}, f32[4,32,6]{1,2,0:T(8,128)}, u32[]{:S(2)}) copy-start(f32[4,32,6]{1,2,0:T(8,128)} %custom-call.26) | copy-start | bytes 9220
  165.8 8.2 %copy-start.5 = (f32[1024,6]{0,1:T(8,128)S(1)}, f32[1024,6]{0,1:T(8,128)}, u32[]{:S(2)}) copy-start(f32[1024,6]{0,1:T(8,128)} %copy.382) | copy-start | bytes 73732
  165.8 8.2 %copy-start.6 = (f32[3,1024]{1,0:T(4,128)S(1)}, f32[3,1024]{1,0:T(4,128)}, u32[]{:S(2)}) copy-start(f32[3,1024]{1,0:T(4,128)} %param.25) | copy-start | bytes 36868
  165.8 8.2 %copy-start.7 = (f32[3,1024]{1,0:T(4,128)S(1)}, f32[3,1024]{1,0:T(4,128)}, u32[]{:S(2)}) copy-start(f32[3,1024]{1,0:T(4,128)} %param.24) | copy-start | bytes 36868
  165.8 8.2 %copy-start.8 = (f32[3,1024]{1,0:T(4,128)S(1)}, f32[3,1024]{1,0:T(4,128)}, u32[]{:S(2)}) copy-start(f32[3,1024]{1,0:T(4,128)} %param.27) | copy-start | bytes 36868
  167.5 2.5 %collective-permute-start.2 = (f32[6,128]{1,0:T(8,128)S(1)}, f32[6,128]{1,0:T(8,128)S(1)}, u32[]{:S(2)}, u32[]{:S(2)}) collective-permute-start(f32[6,128]{1,0:T(8,128)S(1)} %get-tuple-element.461), channel_id=1, source_target_pairs={{0,63},{1,0},{2,1},{3,2},{4,3},{5,4},{6,5},{7,6},{8,7},{9,8},{10,9... | collective-permute-start | bytes 9224 | tf_op jit(solution)/shard_map/ppermute | solution.py:33
  167.5 6.4 %collective-permute-start.3 = (f32[6,128]{1,0:T(8,128)S(1)}, f32[6,128]{1,0:T(8,128)S(1)}, u32[]{:S(2)}, u32[]{:S(2)}) collective-permute-start(f32[6,128]{1,0:T(8,128)S(1)} %get-tuple-element.460), channel_id=1, source_target_pairs={{0,1},{1,2},{2,3},{3,4},{4,5},{5,6},{6,7},{7,8},{8,9},{9,10},{10,1... | collective-permute-start | bytes 9224 | tf_op jit(solution)/shard_map/ppermute | solution.py:33
where the time goes:
time: 176 us; the launch traced here: 175 us
  other arithmetic  82.9 us (47%)
  local copies, waits for them, and re-layouts  60.6 us (34%)
  starting transfers between devices  22.4 us (13%)
  waiting for transfers between devices  6.76 us (4%)
    reduce_sum x6, other arithmetic, tile(): along_j = jnp.sum(pushes, 2)  28 us
    mul x6, other arithmetic, tile(): pushes = magnitude[:, None] * delta  11 us
    sub x6, other arithmetic, tile(): delta = world_i[:, :3, :, None] - world_j[:, :3, None, :]  10.7 us
    gather x8, local copies, waits for them, and re-layouts, fetch_near(): world_j = jnp.take(all_flat, index, 0)  9.57 us
    ppermute x1, starting transfers between devices, with_halo(): after = lax.ppermute(initial, axis, down)  7.49 us
    gather x4, local copies, waits for them, and re-layouts, fetch_near(): centre_j = jnp.take(all_centre, index, 0)  6.64 us
    while x5, local copies, waits for them, and re-layouts, pair_loop(): lax.map(work, (first.reshape(-1, block), second.reshape(-1, block), neck....  6.64 us
    unnamed x44, local copies, waits for them, and re-layouts  5.19 us
  transfers between devices with their start and end apart: 7, of which 3 were waited for; matrix products, arithmetic and copies ran while one was open for 28% of the time, Pallas kernels for 0%

commit v1 on v0

v1 whole, which is shorter than its diff:
```python
import functools
import math

import jax
import jax.numpy as jnp
from jax import lax
from jax.experimental import pallas as pl
from jax.experimental.pallas import tpu as pltpu
from jax.sharding import PartitionSpec as P

F32 = jnp.float32
BF16 = jnp.bfloat16
I32 = jnp.int32

BOUND_DEV = 128
CX = 32
KINDS = 64
SUB = 128
GRAINS_DEV = 1024
LANES = 128
UNIT = 32
PARTS = LANES // UNIT
ROWS = SUB // PARTS

time_step = 0.05
stiffness = 0.0078125
cohesion = 0.05
inertia = 0.4

SCALE = math.sqrt(math.log2(math.e) / 4)
SOFT = 0.01 * SCALE * SCALE
LIFT = 2.0**SOFT
GAIN = LIFT * SCALE * stiffness
BOND = LIFT * SCALE * cohesion
DRAG = LIFT * stiffness


def iota(shape, dim):
    return lax.broadcasted_iota(I32, shape, dim)


def thirds(x):
    hi = x.astype(BF16).astype(F32)
    rest = x - hi
    mid = rest.astype(BF16).astype(F32)
    return jnp.concatenate([hi, mid, rest - mid], 0).astype(BF16)


def joined(y):
    n = y.shape[0] // 3
    return (y[2 * n :] + y[n : 2 * n]) + y[:n]


def dot(a, b):
    return lax.dot_general(a, b, (((1,), (0,)), ((), ())), preferred_element_type=F32)


def dot_t(a, b):
    return lax.dot_general(a, b, (((1,), (1,)), ((), ())), preferred_element_type=F32)


def hot(index, count):
    return jnp.where(iota((count, index.shape[1]), 0) == index, 1.0, 0.0).astype(BF16)


def wide(row):
    return jnp.concatenate([row, jnp.zeros((1, LANES - row.shape[1]), row.dtype)], 1)


def stack(rows, count):
    at = iota((count, rows[0].shape[1]), 0)
    out = jnp.zeros((count, rows[0].shape[1]), F32)
    for k, row in enumerate(rows):
        out = jnp.where(at == k, row, out)
    return out


def compact(actives, fields):
    segments = len(actives)
    flags = stack([a.astype(F32) for a in actives], 16)
    below = jnp.where(iota((LANES, LANES), 0) < iota((LANES, LANES), 1), 1.0, 0.0).astype(BF16)
    inside = dot(flags.astype(BF16), below)
    sums = dot(flags.astype(BF16), jnp.ones((LANES, LANES), BF16))
    ranks = []
    before = jnp.zeros((1, LANES), F32)
    for s in range(segments):
        ranks.append(jnp.where(actives[s], inside[s : s + 1] + before, -1.0).astype(I32))
        before = before + sums[s : s + 1]
    total = jnp.sum(flags).astype(I32)
    parts = thirds(jnp.concatenate([stack(f, 16) for f in fields], 1))
    return jnp.concatenate(ranks, 1), parts, total


def picked(ranks, parts, base):
    want = iota((LANES, ranks.shape[1]), 0) + base
    chosen = jnp.where(want == ranks, 1.0, 0.0).astype(BF16)
    return joined(dot_t(parts, chosen))


def pair_unit(number, pose_ref, table_ref, u_ref, v_ref, both):
    spread = jnp.where(
        iota((LANES, LANES), 0) == number * UNIT + (iota((LANES, LANES), 1) & (UNIT - 1)), 1.0, 0.0
    ).astype(BF16)
    pose = joined(dot(pose_ref[...], spread))
    part = iota((1, LANES), 1) // UNIT
    shift = [SCALE * (pose[c : c + 1] - pose[16 + c : 17 + c]) for c in range(3)]

    def kinds(row):
        at = iota((4 * KINDS, LANES), 0)
        kind = row.astype(I32)
        return jnp.where(((at & (KINDS - 1)) == kind) & (at < 3 * KINDS), 1.0, 0.0).astype(BF16)

    second = dot(table_ref[...], kinds(pose[28:29]))
    for c in range(3):
        turn = [SCALE * pose[16 + 3 + 3 * c + e : 16 + 4 + 3 * c + e] for e in range(3)]
        v_ref[c] = turn[0] * second[:SUB] + turn[1] * second[SUB : 2 * SUB] + turn[2] * second[2 * SUB : 3 * SUB]
    v_ref[3] = GAIN * second[3 * SUB :]

    first = dot(table_ref[...], kinds(pose[12:13]))
    mine = []
    for e in range(4):
        value = first[e * SUB : e * SUB + ROWS]
        for k in range(1, PARTS):
            value = jnp.where(part == k, first[e * SUB + k * ROWS : e * SUB + (k + 1) * ROWS], value)
        mine.append(value)
    for c in range(3):
        turn = [SCALE * pose[3 + 3 * c + e : 4 + 3 * c + e] for e in range(3)]
        u_ref[c] = shift[c] + (turn[0] * mine[0] + turn[1] * mine[1] + turn[2] * mine[2])
    u_ref[3] = GAIN * mine[3] - BOND * pose[13:14]

    blocks = ROWS // 8
    u = [[u_ref[c, 8 * k : 8 * k + 8, :] for c in range(4)] for k in range(blocks)]

    def step(b, sums):
        v = [v_ref[c, pl.ds(b, 8, stride=0), :] for c in range(4)]
        out = []
        for k in range(blocks):
            x, y, z = (u[k][c] - v[c] for c in range(3))
            square = (x * x + SOFT) + y * y + z * z
            m = ((u[k][3] + v[3]) * lax.rsqrt(square) - DRAG) * jnp.exp2(-square)
            s = sums[k]
            out.append((s[0] + m * v[0], s[1] + m * v[1], s[2] + m * v[2], s[3] + m))
        return tuple(out)

    zero = jnp.zeros((8, LANES), F32)
    sums = lax.fori_loop(0, SUB, step, ((zero,) * 4,) * blocks, unroll=4)

    terms = [zero] * 9
    for k in range(blocks):
        z = sums[k][:3]
        g = [sums[k][3] * u[k][c] - z[c] for c in range(3)]
        arm = [u[k][c] - shift[c] for c in range(3)]
        for c in range(3):
            n, o = (c + 1) % 3, (c + 2) % 3
            terms[c] = terms[c] + g[c]
            terms[3 + c] = terms[3 + c] + (arm[n] * g[o] - arm[o] * g[n])
            if both:
                terms[6 + c] = terms[6 + c] - (z[n] * u[k][o] - z[o] * u[k][n])
    rows = [jnp.sum(t, 0, keepdims=True) for t in terms]
    rows = [r * (1 / SCALE if k < 3 else 1 / SCALE**2) for k, r in enumerate(rows)]
    zero_row = jnp.zeros((1, LANES), F32)
    listed = rows[:6] + [zero_row, zero_row]
    if both:
        listed += [-r for r in rows[:3]] + rows[6:]
    return joined(dot_t(thirds(stack(listed, 16)), spread))


def prepare_kernel(
    position_ref, velocity_ref, accel_ref, turn_ref, kind_ref, first_ref, second_ref, neck_ref,
    cross_first_ref, cross_second_ref, cross_neck_ref, export_ref,
    moved_ref, pose_ref, near_ref, far1_ref, far2_ref, far3_ref,
):
    group = lax.axis_index("group")
    moved = position_ref[...] + time_step * velocity_ref[...] + 0.5 * time_step**2 * accel_ref[...]
    moved_ref[...] = moved
    pose_ref[0:3, :] = moved
    pose_ref[3:12, :] = turn_ref[...]
    pose_ref[12:13, :] = kind_ref[...].astype(F32)
    pose_ref[13:16, :] = jnp.zeros((3, GRAINS_DEV), F32)
    index = jnp.concatenate([first_ref[...], wide(cross_first_ref[...]), export_ref[...]], 1)
    got = joined(dot(thirds(pose_ref[...]), hot(index, GRAINS_DEV)))
    at = iota((16, LANES), 0)
    near_ref[0:16, :] = pose_ref[:, :BOUND_DEV]
    listed = jnp.where(at == 13, second_ref[...].astype(F32), got[:, :LANES])
    near_ref[16:32, :] = jnp.where(at == 14, neck_ref[...], listed)
    listed = jnp.where(at == 13, wide(cross_second_ref[...]).astype(F32), got[:, LANES : 2 * LANES])
    listed = jnp.where(at == 14, wide(cross_neck_ref[...]), listed)
    exported = got[:, 2 * LANES :]
    for k, far_ref in ((1, far1_ref), (2, far2_ref), (3, far3_ref)):
        to = (group + k) & 3
        turned = pltpu.roll(exported, (64 - CX * to) & (LANES - 1), 1)
        far_ref[...] = jnp.where(iota((16, LANES), 1) < 64, listed, turned)


def tiles(total, ranks, parts, other_of, poses_ref, table_ref, out_ref, pose_ref, u_ref, v_ref, both):
    def tile(t, carry):
        fields = picked(ranks, parts, t * LANES)
        own = hot(fields[0:1].astype(I32) - 1, GRAINS_DEV)
        mine = joined(dot(poses_ref[...], own))
        mine = jnp.where(iota((16, LANES), 0) == 13, fields[2:3], mine)
        other_index = fields[1:2].astype(I32) - 1
        other = hot(other_index, other_of.shape[1])
        theirs = joined(dot(other_of[...], other))
        pose_ref[...] = thirds(jnp.concatenate([mine, theirs], 0))
        units = jnp.minimum(PARTS, (total - t * LANES + UNIT - 1) // UNIT)
        terms = lax.fori_loop(
            0,
            units,
            lambda n, s: s + pair_unit(n, pose_ref, table_ref, u_ref, v_ref, both),
            jnp.zeros((16, LANES), F32),
        )
        found = joined(dot_t(thirds(terms[:8]), own))
        if both:
            found = found + joined(dot_t(thirds(terms[8:]), other))
        out_ref[...] += found
        return carry

    lax.fori_loop(0, (total + LANES - 1) // LANES, tile, 0)


def local_kernel(
    poses_in_ref, first_ref, second_ref, neck_ref, cross_first_ref, cross_second_ref, cross_neck_ref, export_ref,
    offset_ref, radius_ref,
    out_ref, table_ref,
    poses_ref, pose_ref, u_ref, v_ref,
):
    group = lax.axis_index("group")
    blank = jnp.zeros((LANES - KINDS, SUB), F32)
    for e in range(4):
        rows = radius_ref[...] if e == 3 else offset_ref[:, e, :]
        hi = rows.astype(BF16).astype(F32)
        mid = (rows - hi).astype(BF16).astype(F32)
        low = rows - hi - mid
        table_ref[e * SUB : (e + 1) * SUB, :LANES] = jnp.concatenate([hi, mid], 0).T.astype(BF16)
        table_ref[e * SUB : (e + 1) * SUB, LANES:] = jnp.concatenate([low, blank], 0).T.astype(BF16)
    poses_ref[...] = thirds(poses_in_ref[...])
    out_ref[...] = jnp.zeros_like(out_ref)
    first, second = first_ref[...], second_ref[...]
    cross = wide(cross_second_ref[...])
    ours = (cross >> 5 == group) & (iota((1, LANES), 1) < cross_second_ref.shape[1])
    slot = joined(dot(thirds(stack([export_ref[...].astype(F32)], 16)), hot(cross, LANES)))[0:1]
    partner = (first + 1 + second) & (GRAINS_DEV - 1)
    ranks, parts, total = compact(
        [second < GRAINS_DEV - 1, ours],
        [
            [(first + 1).astype(F32), (partner + 1).astype(F32), neck_ref[...]],
            [(wide(cross_first_ref[...]) + 1).astype(F32), slot + 1, wide(cross_neck_ref[...])],
        ],
    )
    tiles(total, ranks, parts, poses_ref, poses_ref, table_ref, out_ref, pose_ref, u_ref, v_ref, True)


def remote_kernel(
    poses_in_ref, first_ref, second_ref, neck_ref, cross_first_ref, cross_second_ref, cross_neck_ref, export_ref,
    table_ref, local_ref, velocity_ref, accel_ref, spin_ref, before_ref, after_ref, far1_ref, far2_ref, far3_ref,
    velocity_out_ref, spin_out_ref,
    poses_ref, pool_ref, out_ref, pose_ref, u_ref, v_ref,
):
    group = lax.axis_index("group")
    lane = iota((1, LANES), 1)
    poses_ref[...] = thirds(poses_in_ref[...])
    fars = (far1_ref, far2_ref, far3_ref)
    pool = [before_ref[0:16, :], after_ref[0:16, :], before_ref[16:32, :], after_ref[16:32, :]]
    pool_ref[...] = thirds(jnp.concatenate(pool + [f[...] for f in fars], 1))
    out_ref[...] = local_ref[...]
    actives, fields = [], []

    def add(active, own, place, neck):
        actives.append(active)
        fields.append([(own + 1).astype(F32), (place + 1).astype(F32), neck])

    beyond = second_ref[...] - (GRAINS_DEV - 1)
    add(beyond >= 0, first_ref[...], beyond, neck_ref[...])
    cross = wide(cross_second_ref[...])
    way = (group - (cross >> 5)) & 3
    add(
        (way != 0) & (lane < 64),
        wide(cross_first_ref[...]),
        3 * LANES + way * LANES + 64 + (cross & (CX - 1)),
        wide(cross_neck_ref[...]),
    )
    beyond = before_ref[29:30, :].astype(I32) - (GRAINS_DEV - 1)
    add(beyond >= BOUND_DEV, beyond - BOUND_DEV, 2 * LANES + lane, before_ref[30:31, :])
    beyond = after_ref[29:30, :].astype(I32) - (GRAINS_DEV - 1)
    add((beyond >= 0) & (beyond < BOUND_DEV), beyond, 3 * LANES + lane, after_ref[30:31, :])
    exports = thirds(stack([export_ref[...].astype(F32)], 16))
    for k in (1, 2, 3):
        wanted = fars[k - 1][13:14, :].astype(I32)
        sender = (group - k) & 3
        slot = joined(dot(exports, hot(sender * CX + (wanted & (CX - 1)), LANES)))[0:1]
        add(
            (wanted >> 5 == group) & (lane < 64),
            slot,
            (3 + k) * LANES + lane,
            fars[k - 1][14:15, :],
        )
    ranks, parts, total = compact(actives, fields)
    tiles(total, ranks, parts, pool_ref, poses_ref, table_ref, out_ref, pose_ref, u_ref, v_ref, False)
    velocity_out_ref[...] = velocity_ref[...] + 0.5 * time_step * (accel_ref[...] + out_ref[0:3, :])
    spin_out_ref[...] = spin_ref[...] + time_step * out_ref[3:6, :] / inertia


def shifted(array, axis, by):
    devices = lax.axis_size(axis)
    return lax.ppermute(array, axis, [(i, (i + by) % devices) for i in range(devices)])


def shape(rows, columns, kind=F32):
    return jax.ShapeDtypeStruct((rows, columns), kind)


def on_device(
    position, velocity, accel_old, orientation, spin, shape_index, shape_offsets, shape_radii,
    pair_first, pair_second, pair_neck, cross_first, cross_second, cross_neck, export_slots,
):
    row = lambda x: x.reshape(1, x.shape[0])
    lists = [row(x) for x in (pair_first, pair_second, pair_neck, cross_first, cross_second, cross_neck, export_slots)]
    moved, poses, near, far1, far2, far3 = pl.pallas_call(
        prepare_kernel,
        out_shape=(
            shape(3, GRAINS_DEV), shape(16, GRAINS_DEV), shape(32, LANES),
            shape(16, LANES), shape(16, LANES), shape(16, LANES),
        ),
        compiler_params=pltpu.CompilerParams(vmem_limit_bytes=48 << 20),
        name="prepare",
    )(position, velocity, accel_old, orientation, row(shape_index), *lists)
    before = shifted(near, "region", 1)
    after = shifted(near, "region", -1)
    fars = [shifted(f, "group", k) for k, f in ((1, far1), (2, far2), (3, far3))]
    work = [
        pltpu.VMEM((96, LANES), BF16),
        pltpu.VMEM((4, ROWS, LANES), F32),
        pltpu.VMEM((4, SUB, LANES), F32),
    ]
    local, table = pl.pallas_call(
        local_kernel,
        out_shape=(shape(8, GRAINS_DEV), shape(4 * SUB, 4 * KINDS, BF16)),
        scratch_shapes=[pltpu.VMEM((48, GRAINS_DEV), BF16)] + work,
        compiler_params=pltpu.CompilerParams(vmem_limit_bytes=48 << 20),
        cost_estimate=pl.CostEstimate(flops=4_000_000_000, bytes_accessed=1_000_000, transcendentals=4_000_000),
        name="local",
    )(poses, *lists, shape_offsets, shape_radii)
    velocity_new, spin_new = pl.pallas_call(
        remote_kernel,
        out_shape=(shape(3, GRAINS_DEV), shape(3, GRAINS_DEV)),
        scratch_shapes=[
            pltpu.VMEM((48, GRAINS_DEV), BF16), pltpu.VMEM((48, 7 * LANES), BF16), pltpu.VMEM((8, GRAINS_DEV), F32)
        ] + work,
        compiler_params=pltpu.CompilerParams(vmem_limit_bytes=48 << 20),
        name="remote",
    )(poses, *lists, table, local, velocity, accel_old, spin, before, after, *fars)
    return (moved, velocity_new, spin_new)


def solution(mesh):
    both = ("group", "region")
    wide_spec, flat = P(None, both), P(both)
    return jax.shard_map(
        on_device,
        mesh=mesh,
        in_specs=(wide_spec,) * 5 + (flat, P(), P()) + (flat,) * 7,
        out_specs=(wide_spec,) * 3,
        check_vma=False,
    )
```

time: 176 us -> 44.2 us (0.25)
  other arithmetic: 82.9 us -> 0 us
  local copies, waits for them, and re-layouts: 60.6 us -> 3.79 us
  Pallas kernels: 0 us -> 26.6 us
  starting transfers between devices: 22.4 us -> 12.4 us
  waiting for transfers between devices: 6.76 us -> 0.01 us
    gather x33 -> x0, local copies, waits for them, and re-layouts: 32.2 us -> none  [the longest x8 9.57 us: fetch_near(): world_j = jnp.take(all_flat, index, 0)]
    reduce_sum x18 -> x0, other arithmetic: 29.4 us -> none  [the longest x6 28 us: tile(): along_j = jnp.sum(pushes, 2)]
    pallas_call x0 -> x3, Pallas kernels: none -> 26.6 us  [the longest x1 14.7 us: on_device(): pl.pallas_call(remote_kernel, out_shape=(shape(3, GRAINS_DEV), shape(3, G...]
    all_to_all x3 -> x0, starting transfers between devices: 14.4 us -> none  [the longest x1 4.91 us: on_device(): lax.all_to_all(sent_kinds, 'group', split_axis=0, concat_axis=0, tiled=True)]
    mul x12 -> x0, other arithmetic: 13.7 us -> none  [the longest x6 11 us: tile(): pushes = magnitude[:, None] * delta]
    sub x24 -> x0, other arithmetic: 12.1 us -> none  [the longest x6 10.7 us: tile(): delta = world_i[:, :3, :, None] - world_j[:, :3, None, :]]
    while x5 -> x0, local copies, waits for them, and re-layouts: 6.64 us -> none  [pair_loop(): lax.map(work, (first.reshape(-1, block), second.reshape(-1, block), neck....]
    select_n x37 -> x0, other arithmetic: 5.76 us -> none  [the longest x8 3.18 us: fetch_near(): world_j = jnp.take(all_flat, index, 0)]
  transfers between devices with their start and end apart: 7 -> 5, of which waited for: 3 -> 0; matrix products, arithmetic and copies ran while one was open for 28% -> 0% of each run, Pallas kernels for 0% -> 25%
where the time goes in v1:
time: 44.2 us; the launch traced here: 43.6 us
  Pallas kernels  26.6 us (60%)
  starting transfers between devices  12.4 us (28%)
  local copies, waits for them, and re-layouts  3.79 us (9%)
  between operations  0.82 us (2%)
    pallas_call x1, Pallas kernels, on_device(): pl.pallas_call(remote_kernel, out_shape=(shape(3, GRAINS_DEV), shape(3, G...  14.7 us
    ppermute x5, starting transfers between devices, shifted(): lax.ppermute(array, axis, [(i, (i + by) % devices) for i in range(devices)])  12.4 us
    pallas_call x1, Pallas kernels, on_device(): pl.pallas_call(local_kernel, out_shape=(shape(8, GRAINS_DEV), shape(4 * S...  11 us
    unnamed x35, local copies, waits for them, and re-layouts  3.79 us
  transfers between devices with their start and end apart: 5, of which 0 were waited for; matrix products, arithmetic and copies ran while one was open for 0% of the time, Pallas kernels for 25%

profile of v1, /device:TPU:8, one launch (start us, length us, event | category | flops | bytes accessed | tf_op | source)
XLA Modules:
  0.0 43.6 jit_solution(10135130841021861151)
XLA Ops:
  0.6 0.0 copy-start.7
  0.6 0.0 copy-start.11
  0.7 0.0 copy-start.12
  0.7 0.0 copy-start.13
  0.7 0.0 copy-start.14
  0.7 0.0 copy-start.8
  0.7 0.0 copy-start.9
  0.7 0.0 copy-start.10
  0.7 0.6 %copy-done.7 = s32[1024]{0:T(1024)S(1)} copy-done((s32[1024]{0:T(1024)S(1)}, s32[1024]{0:T(1024)}, u32[]{:S(2)}) %copy-start.7) | copy-done | bytes 4120
  1.3 0.0 copy-done.11
  1.3 0.0 copy-done.12
  1.3 0.0 copy-done.13
  1.3 0.0 copy-done.14
  1.4 0.0 copy-done.8
  1.4 0.0 copy-done.9
  1.4 0.0 copy-done.10
  1.4 0.0 copy-start
  1.4 0.8 %copy-done = f32[9,1024]{1,0:T(8,128)S(1)} copy-done((f32[9,1024]{1,0:T(8,128)S(1)}, f32[9,1024]{1,0:T(8,128)}, u32[]{:S(2)}) %copy-start) | copy-done | bytes 36888
  2.2 0.0 copy-start.1
  2.2 0.7 %copy-done.1 = f32[3,1024]{1,0:T(4,128)S(1)} copy-done((f32[3,1024]{1,0:T(4,128)S(1)}, f32[3,1024]{1,0:T(4,128)}, u32[]{:S(2)}) %copy-start.1) | copy-done | bytes 12312
  3.0 0.0 copy-start.3
  3.0 0.7 %copy-done.3 = f32[3,1024]{1,0:T(4,128)S(1)} copy-done((f32[3,1024]{1,0:T(4,128)S(1)}, f32[3,1024]{1,0:T(4,128)}, u32[]{:S(2)}) %copy-start.3) | copy-done | bytes 12312
  3.7 0.0 copy-start.6
  3.7 0.7 %copy-done.6 = f32[3,1024]{1,0:T(4,128)S(1)} copy-done((f32[3,1024]{1,0:T(4,128)S(1)}, f32[3,1024]{1,0:T(4,128)}, u32[]{:S(2)}) %copy-start.6) | copy-done | bytes 12312
  4.4 0.0 copy-start.16
  4.4 0.9 %prepare.1 = (f32[3,1024]{1,0:T(4,128)}, f32[16,1024]{1,0:T(8,128)S(1)}, f32[32,128]{1,0:T(8,128)S(1)}, f32[16,128]{1,0:T(8,128)S(1)}, f32[16,128]{1,0:T(8,128)S(1)}, /*index=5*/f32[16,128]{1,0:T(8,128)S(1)}) custom-call(f32[3,1024]{1,0:T(4,128)S(1)} %copy-done.6, f32[3,1024]{1,0:T(4,128)S(1)} %copy-done.1, f32[3,1024]{1,0:T(4,128)S(1)} %copy-done.3, ...), custom_call_target="tpu_custom_call" | custom-call | tf_op jit(solution)/shard_map/prepare/pallas_call | solution.py:318
  5.3 0.0 collective-permute-start
  5.3 7.5 %collective-permute-start.1 = (f32[32,128]{1,0:T(8,128)S(1)}, f32[32,128]{1,0:T(8,128)S(1)}, u32[]{:S(2)}, u32[]{:S(2)}) collective-permute-start(f32[32,128]{1,0:T(8,128)S(1)} %get-tuple-element.17), channel_id=1, source_target_pairs={{0,63},{1,0},{2,1},{3,2},{4,3},{5,4},{6,5},{7,6},{8,7},{9,8},{10,9... | collective-permute-start | bytes 49160 | tf_op jit(solution)/shard_map/ppermute | solution.py:305
  12.7 1.6 %collective-permute-start.2 = (f32[16,128]{1,0:T(8,128)S(1)}, f32[16,128]{1,0:T(8,128)S(1)}, u32[]{:S(2)}, u32[]{:S(2)}) collective-permute-start(f32[16,128]{1,0:T(8,128)S(1)} %get-tuple-element.18), channel_id=1, source_target_pairs={{0,64},{64,128},{128,192},{192,0},{1,65},{65,129},{129,193},{193,1... | collective-permute-start | bytes 24584 | tf_op jit(solution)/shard_map/ppermute | solution.py:305
  14.3 0.9 %collective-permute-start.3 = (f32[16,128]{1,0:T(8,128)S(1)}, f32[16,128]{1,0:T(8,128)S(1)}, u32[]{:S(2)}, u32[]{:S(2)}) collective-permute-start(f32[16,128]{1,0:T(8,128)S(1)} %get-tuple-element.19), channel_id=1, source_target_pairs={{0,128},{64,192},{128,0},{192,64},{1,129},{65,193},{129,1},{193,65... | collective-permute-start | bytes 24584 | tf_op jit(solution)/shard_map/ppermute | solution.py:305
  15.3 0.0 copy-start.15
  15.3 2.4 %collective-permute-start.4 = (f32[16,128]{1,0:T(8,128)S(1)}, f32[16,128]{1,0:T(8,128)S(1)}, u32[]{:S(2)}, u32[]{:S(2)}) collective-permute-start(f32[16,128]{1,0:T(8,128)S(1)} %get-tuple-element.20), channel_id=1, source_target_pairs={{0,192},{64,0},{128,64},{192,128},{1,193},{65,1},{129,65},{193,129... | collective-permute-start | bytes 24584 | tf_op jit(solution)/shard_map/ppermute | solution.py:305
  17.7 0.0 copy-done.16
  17.7 0.1 copy.18.offset_ref
  17.8 0.0 copy-done.15
  17.8 0.0 copy-start.2
  17.8 0.0 copy-start.4
  17.8 0.0 copy-start.5
  17.8 11.0 %local.1 = (f32[8,1024]{1,0:T(8,128)S(1)}, bf16[512,256]{1,0:T(8,128)(2,1)S(1)}) custom-call(f32[16,1024]{1,0:T(8,128)S(1)} %get-tuple-element.14.poses_in_ref, s32[1,128]{1,0:T(1,128)S(1)} %bitcast.10, s32[1,128]{1,0:T(1,128)S(1)} %bitcast.13, f32[1,128]{1,0:T(1,128)S(1)} %bitcast.16, s32[1,64]{1,0:T(1,128)S(1)} %bitcast.19, s32[1,64]{1,0:T(1,128)S(1)} %bitcast.22, ...), custom_call_target="tpu_custom_call" | custom-call | flops 4000000000 | bytes 1000000 | tf_op jit(solution)/shard_map/local/pallas_call | solution.py:335
  28.8 0.0 collective-permute-done.2.far1_ref
  28.8 0.0 collective-permute-done.3.far2_ref
  28.9 0.0 collective-permute-done.4.far3_ref
  28.9 0.0 collective-permute-done.before_ref
  28.9 0.0 collective-permute-done.1.after_ref
  28.9 0.0 copy-done.2
  28.9 0.0 copy-done.4
  28.9 0.0 copy-done.5
  28.9 14.7 %remote.1 = (f32[3,1024]{1,0:T(4,128)}, f32[3,1024]{1,0:T(4,128)}) custom-call(f32[16,1024]{1,0:T(8,128)S(1)} %get-tuple-element.14.poses_in_ref, s32[1,128]{1,0:T(1,128)S(1)} %bitcast.11, s32[1,128]{1,0:T(1,128)S(1)} %bitcast.14, f32[1,128]{1,0:T(1,128)S(1)} %bitcast.17, s32[1,64]{1,0:T(1,128)S(1)} %bitcast.20, s32[1,64]{1,0:T(1,128)S(1)} %bitcast.23, ...), custom_call_target="tpu_custom_call" | custom-call | tf_op jit(solution)/shard_map/remote/pallas_call | solution.py:343
Async XLA Ops:
  0.6 0.7 %copy-start.7 = (s32[1024]{0:T(1024)S(1)}, s32[1024]{0:T(1024)}, u32[]{:S(2)}) copy-start(s32[1024]{0:T(1024)} %param.20) | copy-start | bytes 12292
  0.6 0.7 %copy-start.11 = (s32[64]{0:T(128)S(1)}, s32[64]{0:T(128)}, u32[]{:S(2)}) copy-start(s32[64]{0:T(128)} %param.26) | copy-start | bytes 772
  0.7 0.7 %copy-start.12 = (s32[64]{0:T(128)S(1)}, s32[64]{0:T(128)}, u32[]{:S(2)}) copy-start(s32[64]{0:T(128)} %param.27) | copy-start | bytes 772
  0.7 0.7 %copy-start.13 = (f32[64]{0:T(128)S(1)}, f32[64]{0:T(128)}, u32[]{:S(2)}) copy-start(f32[64]{0:T(128)} %param.28) | copy-start | bytes 772
  0.7 0.7 %copy-start.14 = (s32[128]{0:T(128)S(1)}, s32[128]{0:T(128)}, u32[]{:S(2)}) copy-start(s32[128]{0:T(128)} %param.29) | copy-start | bytes 1540
  0.7 0.7 %copy-start.8 = (s32[128]{0:T(128)S(1)}, s32[128]{0:T(128)}, u32[]{:S(2)}) copy-start(s32[128]{0:T(128)} %param.23) | copy-start | bytes 1540
  0.7 0.7 %copy-start.9 = (s32[128]{0:T(128)S(1)}, s32[128]{0:T(128)}, u32[]{:S(2)}) copy-start(s32[128]{0:T(128)} %param.24) | copy-start | bytes 1540
  0.7 0.7 %copy-start.10 = (f32[128]{0:T(128)S(1)}, f32[128]{0:T(128)}, u32[]{:S(2)}) copy-start(f32[128]{0:T(128)} %param.25) | copy-start | bytes 1540
  1.4 0.8 %copy-start = (f32[9,1024]{1,0:T(8,128)S(1)}, f32[9,1024]{1,0:T(8,128)}, u32[]{:S(2)}) copy-start(f32[9,1024]{1,0:T(8,128)} %turn_ref.1) | copy-start | bytes 110596
  2.2 0.7 %copy-start.1 = (f32[3,1024]{1,0:T(4,128)S(1)}, f32[3,1024]{1,0:T(4,128)}, u32[]{:S(2)}) copy-start(f32[3,1024]{1,0:T(4,128)} %velocity_ref.3) | copy-start | bytes 36868
  3.0 0.7 %copy-start.3 = (f32[3,1024]{1,0:T(4,128)S(1)}, f32[3,1024]{1,0:T(4,128)}, u32[]{:S(2)}) copy-start(f32[3,1024]{1,0:T(4,128)} %accel_ref.3) | copy-start | bytes 36868
  3.7 0.7 %copy-start.6 = (f32[3,1024]{1,0:T(4,128)S(1)}, f32[3,1024]{1,0:T(4,128)}, u32[]{:S(2)}) copy-start(f32[3,1024]{1,0:T(4,128)} %position_ref.1) | copy-start | bytes 36868
  4.4 13.3 %copy-start.16 = (f32[64,3,128]{2,0,1:T(8,128)S(1)}, f32[64,3,128]{2,0,1:T(8,128)}, u32[]{:S(2)}) copy-start(f32[64,3,128]{2,0,1:T(8,128)} %param.21) | copy-start | bytes 294916
  5.3 23.6 %collective-permute-start = (f32[32,128]{1,0:T(8,128)S(1)}, f32[32,128]{1,0:T(8,128)S(1)}, u32[]{:S(2)}, u32[]{:S(2)}) collective-permute-start(f32[32,128]{1,0:T(8,128)S(1)} %get-tuple-element.17), channel_id=1, source_target_pairs={{0,1},{1,2},{2,3},{3,4},{4,5},{5,6},{6,7},{7,8},{8,9},{9,10},{10,1... | collective-permute-start | bytes 49160 | tf_op jit(solution)/shard_map/ppermute | solution.py:305
  5.3 23.6 %collective-permute-start.1 = (f32[32,128]{1,0:T(8,128)S(1)}, f32[32,128]{1,0:T(8,128)S(1)}, u32[]{:S(2)}, u32[]{:S(2)}) collective-permute-start(f32[32,128]{1,0:T(8,128)S(1)} %get-tuple-element.17), channel_id=1, source_target_pairs={{0,63},{1,0},{2,1},{3,2},{4,3},{5,4},{6,5},{7,6},{8,7},{9,8},{10,9... | collective-permute-start | bytes 49160 | tf_op jit(solution)/shard_map/ppermute | solution.py:305
  12.7 16.1 %collective-permute-start.2 = (f32[16,128]{1,0:T(8,128)S(1)}, f32[16,128]{1,0:T(8,128)S(1)}, u32[]{:S(2)}, u32[]{:S(2)}) collective-permute-start(f32[16,128]{1,0:T(8,128)S(1)} %get-tuple-element.18), channel_id=1, source_target_pairs={{0,64},{64,128},{128,192},{192,0},{1,65},{65,129},{129,193},{193,1... | collective-permute-start | bytes 24584 | tf_op jit(solution)/shard_map/ppermute | solution.py:305
  14.3 14.5 %collective-permute-start.3 = (f32[16,128]{1,0:T(8,128)S(1)}, f32[16,128]{1,0:T(8,128)S(1)}, u32[]{:S(2)}, u32[]{:S(2)}) collective-permute-start(f32[16,128]{1,0:T(8,128)S(1)} %get-tuple-element.19), channel_id=1, source_target_pairs={{0,128},{64,192},{128,0},{192,64},{1,129},{65,193},{129,1},{193,65... | collective-permute-start | bytes 24584 | tf_op jit(solution)/shard_map/ppermute | solution.py:305
  15.3 2.5 %copy-start.15 = (f32[64,128]{1,0:T(8,128)S(1)}, f32[64,128]{1,0:T(8,128)}, u32[]{:S(2)}) copy-start(f32[64,128]{1,0:T(8,128)} %radius_ref.1) | copy-start | bytes 98308
  15.3 13.6 %collective-permute-start.4 = (f32[16,128]{1,0:T(8,128)S(1)}, f32[16,128]{1,0:T(8,128)S(1)}, u32[]{:S(2)}, u32[]{:S(2)}) collective-permute-start(f32[16,128]{1,0:T(8,128)S(1)} %get-tuple-element.20), channel_id=1, source_target_pairs={{0,192},{64,0},{128,64},{192,128},{1,193},{65,1},{129,65},{193,129... | collective-permute-start | bytes 24584 | tf_op jit(solution)/shard_map/ppermute | solution.py:305
  17.8 11.1 %copy-start.2 = (f32[3,1024]{1,0:T(4,128)S(1)}, f32[3,1024]{1,0:T(4,128)}, u32[]{:S(2)}) copy-start(f32[3,1024]{1,0:T(4,128)} %velocity_ref.3) | copy-start | bytes 36868
  17.8 11.1 %copy-start.4 = (f32[3,1024]{1,0:T(4,128)S(1)}, f32[3,1024]{1,0:T(4,128)}, u32[]{:S(2)}) copy-start(f32[3,1024]{1,0:T(4,128)} %accel_ref.3) | copy-start | bytes 36868
  17.8 11.1 %copy-start.5 = (f32[3,1024]{1,0:T(4,128)S(1)}, f32[3,1024]{1,0:T(4,128)}, u32[]{:S(2)}) copy-start(f32[3,1024]{1,0:T(4,128)} %spin_ref.1) | copy-start | bytes 36868
